TPU v7x, 256 devices: a whole 4x4x8 slice. The times are simulated.
256 devices in a mesh: segment: 16 (over x_hi, y, core), expert: 16 (over x_lo, z).
Axes of the slice: x: 4 (x_hi: 2, x_lo: 2; x = x_hi * 2 + x_lo), y: 4, z: 8, core: 2. Of those that a mesh axis runs over, the one named last changes fastest.
Arguments:
- fwd_tokens: bfloat16 [16, 2048, 2048], P('segment', 'expert'), may hold values from -6 to 6
- fwd_routes: int32 [16, 2048, 2], P('segment', 'expert'), may hold values from 0 to 15, all different within a row; in each aligned block of 128 rows (0 to 127, 128 to 255, ..., all dimensions but the last counted through in order) at most 32 rows name the same one
- fwd_weights: float32 [16, 2048, 2], P('segment', 'expert'), may hold values from 0.2 to 1
- saved_tokens: bfloat16 [16, 2048, 2048], P('segment', 'expert'), may hold values from -6 to 6
- bwd_routes: int32 [16, 2048, 2], P('segment', 'expert'), may hold values from 0 to 15, all different within a row; in each aligned block of 128 rows (0 to 127, 128 to 255, ..., all dimensions but the last counted through in order) at most 32 rows name the same one
- bwd_weights: float32 [16, 2048, 2], P('segment', 'expert'), may hold values from 0.2 to 1
- incoming_grad: bfloat16 [16, 2048, 2048], P('segment', 'expert'), may hold values from -6 to 6
- norm_gain: float32 [16, 2048], P('segment'), may hold values from 0.1 to 1.9
- gate_proj: bfloat16 [16, 16, 2048, 768], P('segment', 'expert'), may hold values from -0.125 to 0.125
- up_proj: bfloat16 [16, 16, 2048, 768], P('segment', 'expert'), may hold values from -0.125 to 0.125
- down_proj: bfloat16 [16, 16, 768, 2048], P('segment', 'expert'), may hold values from -0.21875 to 0.21875
Outputs:
- next_input: bfloat16 [16, 2048, 2048], P('segment', 'expert')
- next_grad: bfloat16 [16, 2048, 2048], P('segment', 'expert')
- combine_grad: bfloat16 [16, 2048, 2], P('segment', 'expert')
Inputs may be any that keep to these rules, and one draw needn't show every extreme that they name: `fwd_routes`: each token names 2 different experts. In each aligned block of 128 rows of a section (the rows of one device), no expert is named more than 32 times, and in every draw some expert is named exactly 32 times in some block. `bwd_routes`: as for fwd_routes.
All inputs are finite; a program needn't handle non-finite values.
Results may differ from a plain program's by a relative error of at most 0.012.
Values may be sent and summed in bfloat16 or wider, within the bound.
A program may use at most 128 MiB of HBM per device.

v0:
```python
import functools

import jax
import jax.numpy as jnp
from jax import lax
from jax.experimental import pallas as pl
from jax.experimental.pallas import tpu as pltpu
from jax.sharding import PartitionSpec as P

EPS = 1e-06
MESH = pl.DeviceIdType.MESH
F32 = jnp.float32
BF16 = jnp.bfloat16
SLOTS = 32
TOK = 128
RING = 8
TIERS = ((96, 96, 80, SLOTS), (TOK, TOK, 3 * SLOTS, SLOTS))
SAVED, GRAD, FWD = 0, 1, 2
BWD_ROUTE, FWD_ROUTE = 0, 1
PIECES = 4
GROUPS = (("expert", 1, 16), ("segment", 1, 16))
LAST = 7


def block_of(way, hop):
    return LAST if hop == 4 else 3 * way + hop


def iota(shape, dim):
    return lax.broadcasted_iota(jnp.int32, shape, dim)


def dot(a, b):
    return jnp.dot(a, b, preferred_element_type=F32)


def dot_t(a, b):
    return lax.dot_general(a, b, (((1,), (1,)), ((), ())), preferred_element_type=F32)


def place_of(route, z, x):
    offset = jnp.bitwise_and(route - z + RING, RING - 1)
    return offset, jnp.where(jnp.right_shift(route, 3) != x, 1, 0)


def hops_of(route, forth, z, x):
    offset, other = place_of(route, z, x)
    half = offset == RING // 2
    forth = other == 0 if forth is None else forth == 1
    plus = jnp.where(offset < RING // 2, offset, jnp.where(half & forth, RING // 2, 0))
    minus = jnp.where(offset > RING // 2, RING - offset, jnp.where(half & jnp.logical_not(forth), RING // 2, 0))
    return (plus, minus), other, offset


def partners(axis, stride, count):
    index = lax.axis_index(axis)
    digit = lax.rem(index // stride, count)
    return [{axis: index + (lax.rem(digit + step, count) - digit) * stride} for step in range(1, count)]


def agree(routes_b, routes_f, plan, tier, held, send, recv):
    me = lax.axis_index("expert")
    z, x = lax.rem(me, RING), me // RING
    groups = [partners(*group) for group in GROUPS]
    barrier = pltpu.get_barrier_semaphore()
    for group in groups:
        for peer in group:
            pl.semaphore_signal(barrier, inc=1, device_id=peer, device_id_type=MESH)

    row = iota((8, 1), 0)
    cap = [jnp.zeros((8, 1), F32), jnp.zeros((8, 1), F32)]
    for hop in range(4):
        for i in range(1):
            cap[i] = jnp.where(jnp.bitwise_and(row, 3) == hop, float(TIERS[i][hop]), cap[i])
    need = jnp.zeros((1, 1), F32)
    ways = []
    for routes in (routes_b, routes_f):
        places = [place_of(routes[k : k + 1, :], z, x) for k in range(2)]
        base = [jnp.zeros((1, TOK), jnp.int32)] * 2
        for offset, _ in places:
            base[0] = jnp.maximum(base[0], jnp.where(offset < 4, offset, 0))
            base[1] = jnp.maximum(base[1], jnp.where(offset > 4, RING - offset, 0))
        best = None
        for option in range(4):
            forths, far = [], list(base)
            for k in range(2):
                offset, other = places[k]
                beside = places[1 - k][0]
                free = jnp.where(other == 0, option % 2, option // 2)
                forth = jnp.where((beside > 0) & (beside < 4), 1, jnp.where(beside > 4, 0, free))
                far[0] = jnp.where((offset == 4) & (forth == 1), 4, far[0])
                far[1] = jnp.where((offset == 4) & (forth == 0), 4, far[1])
                forths.append(forth)
            reach = jnp.where(iota((8, TOK), 0) < 4, far[0], far[1])
            goes = jnp.where(reach > jnp.bitwise_and(iota((8, TOK), 0), 3), 1.0, 0.0)
            count = jnp.sum(goes, axis=1, keepdims=True)
            over = [jnp.sum(jnp.maximum(count - c, 0.0), axis=0, keepdims=True) for c in cap]
            score = over[1] * 65536.0 + over[0] * 1024.0 + jnp.sum(count, axis=0, keepdims=True)
            if best is None:
                best = (score, over, forths)
            else:
                take = score < best[0]
                best = (
                    jnp.where(take, score, best[0]),
                    [jnp.where(take, new, old) for new, old in zip(over, best[1])],
                    [jnp.where(take, new, old) for new, old in zip(forths, best[2])],
                )
        own = jnp.where(best[1][0] > 0, 1.0, 0.0)
        need = jnp.maximum(need, own)
        ways += best[2]
    rows = iota((8, TOK), 0)
    table = jnp.zeros((8, TOK), jnp.int32)
    for i, way in enumerate(ways):
        table = jnp.where(rows == i, way, table)
    plan[...] = table

    pl.semaphore_wait(barrier, sum(len(group) for group in groups))
    total = jnp.broadcast_to(need, (8, TOK))
    for i, group in enumerate(groups):
        held[i, 0] = total
        copies = [
            pltpu.make_async_remote_copy(
                src_ref=held.at[i, 0], dst_ref=held.at[i, step + 1], send_sem=send.at[i, step],
                recv_sem=recv.at[i, step], device_id=peer, device_id_type=MESH,
            )
            for step, peer in enumerate(group)
        ]
        for copy in copies:
            copy.start()
        for step, copy in enumerate(copies):
            copy.wait_recv()
            total = jnp.maximum(total, held[i, step + 1])
        for copy in copies:
            copy.wait_send()
    tier[...] = total.astype(jnp.int32)


def code_of(hop, other):
    return jnp.where(hop > 0, 2 * (hop - 1) + other, -1)


def selector(meta, row):
    slot = iota((SLOTS, TOK), 0).astype(F32) + 1.0
    own = jnp.where(slot == meta[row : row + 1, :], 1.0, 0.0)
    other = jnp.where(slot == meta[row + 1 : row + 2, :], 1.0, 0.0)
    return own, other


def spreader(meta, row):
    own, other = selector(meta, row)
    w_own, w_other = meta[row + 2 : row + 3, :], meta[row + 3 : row + 4, :]
    hi_own, hi_other = w_own.astype(BF16).astype(F32), w_other.astype(BF16).astype(F32)
    stacked = jnp.concatenate(
        [own * hi_own, other * hi_other, own * (w_own - hi_own), other * (w_other - hi_other)], axis=0
    )
    return jnp.transpose(stacked).astype(BF16)


def kernel(
    reach, general, plan_ref, tokens_f_hbm, routes_f, weights_f, tokens_b_hbm, routes_b, weights_b, grads_hbm, gain,
    gate_hbm, up_hbm, down_hbm,
    next_input, next_grad, combine,
    tokens_f, tokens_b, grads, packed, r1, r2, r3, r4, meta0, meta1, meta2, meta3, meta4, meta_here, back,
    xsend, xin, w_gate, w_up, w_down, hid_a, hid_b, y_b, y_f, yx_b, yx_f,
    t1, t2, t3, t4, ct_out, ct_in, res, done_f, done_b,
    d_send, d_recv, m_send, m_recv, x_send, x_recv, y_send, y_recv, t_send, t_recv, c_send, c_recv, s_send, s_recv, w_sem,
):
    me = lax.axis_index("expert")
    z, x = lax.rem(me, RING), me // RING
    seg = lax.axis_index("segment")
    sections = lax.axis_size("segment")
    ahead = {"expert": x * RING + lax.rem(z + 1, RING)}
    behind = {"expert": x * RING + lax.rem(z + RING - 1, RING)}
    across = {"expert": (1 - x) * RING + z}
    seg_next = {"segment": lax.rem(seg + 1, sections)}
    seg_prev = {"segment": lax.rem(seg + sections - 1, sections)}
    onward, homeward = (ahead, behind), (behind, ahead)
    width = tokens_f.shape[1]
    hidden = w_gate.shape[1]
    tile = 512
    tiles = width // tile

    loads = [
        pltpu.make_async_copy(src, dst, w_sem.at[i])
        for i, (src, dst) in enumerate(
            (
                (grads_hbm, grads), (tokens_b_hbm, tokens_b), (tokens_f_hbm, tokens_f),
                (gate_hbm, w_gate), (up_hbm, w_up), (down_hbm, w_down),
            )
        )
    ]
    for load in loads:
        load.start()
    barrier = pltpu.get_barrier_semaphore()
    for device in (ahead, behind, across, seg_next, seg_prev):
        pl.semaphore_signal(barrier, inc=1, device_id=device, device_id_type=MESH)

    def over_tiles(body, size=tile):
        @pl.loop(0, width // size)
        def _(i):
            body(pl.ds(pl.multiple_of(i * size, size), size))

    landing = {1: r1, 2: r2, 3: r3}
    returning = {1: t1, 2: t2, 3: t3}
    metas = (meta0, meta1, meta2, meta3, meta4)

    def landed(array, way, hop):
        if hop == 4:
            return r4.at[array, pl.ds(way * SLOTS, SLOTS)]
        return landing[hop].at[array, way]

    def returned(array, way, hop):
        if hop == 4:
            return t4.at[array, pl.ds(way * SLOTS, SLOTS)]
        return returning[hop].at[array, way]

    def remote(src, dst, send, recv, device):
        return pltpu.make_async_remote_copy(
            src_ref=src, dst_ref=dst, send_sem=send, recv_sem=recv, device_id=device, device_id_type=MESH
        )

    def dispatch(array, way, hop):
        source = packed.at[array, way] if hop == 1 else landing[hop - 1].at[array, way]
        rows = reach[hop - 1]
        at = (array, way, hop - 1)
        return remote(
            source.at[pl.ds(0, rows)], landed(array, way, hop), d_send.at[at], d_recv.at[at], onward[way]
        )

    def meta_copy(route, way, hop):
        at = (route, way, hop - 1)
        return remote(
            metas[hop - 1].at[route, way], metas[hop].at[route, way], m_send.at[at], m_recv.at[at], onward[way]
        )

    def cross(array, block):
        here = pl.ds(block * SLOTS, SLOTS)
        there = pl.ds((8 + block) * SLOTS, SLOTS)
        at = (array, block)
        return remote(xsend.at[array, here], xin.at[array, there], x_send.at[at], x_recv.at[at], across)

    outs, outs_x = (y_b, y_f), (yx_b, yx_f)

    def cross_back(which, block):
        there = pl.ds(block * SLOTS, SLOTS)
        here = pl.ds((8 + block) * SLOTS, SLOTS)
        at = (which, block)
        return remote(
            outs[which].at[here], outs_x[which].at[there], y_send.at[at], y_recv.at[at], across
        )

    reused = (SAVED, FWD)

    def piece_of(piece):
        return pl.ds(piece * (width // PIECES), width // PIECES)

    def give_back(which, way, hop, piece):
        at = (which, way, hop - 1, piece)
        cols = piece_of(piece)
        return remote(
            landed(reused[which], way, hop).at[:, cols], returned(which, way, hop).at[:, cols],
            t_send.at[at], t_recv.at[at], homeward[way],
        )

    def give_scalars(way, hop):
        at = (way, hop - 1)
        return remote(ct_out.at[at], ct_in.at[at], c_send.at[at], c_recv.at[at], homeward[way])

    lane = iota((TOK, TOK), 1)
    sub = iota((TOK, TOK), 0)

    def columns_of(rows):
        stacked = jnp.zeros((TOK, TOK), F32)
        for k, row in enumerate(rows):
            stacked = jnp.where(sub == k, row.astype(F32), stacked)
        turned = jnp.transpose(stacked)
        return [turned[:, k : k + 1].astype(jnp.int32) for k in range(len(rows))]

    def forths_of(route):
        return [None if general else plan_ref[2 * route + k : 2 * route + k + 1, :] for k in range(2)]

    def route_columns(r_row, f_row):
        if general:
            return columns_of(r_row), f_row
        columns = columns_of(r_row + f_row)
        return columns[:2], columns[2:]

    def plan(route, routes_ref, weights_ref):
        r_row = [routes_ref[k : k + 1, :] for k in range(2)]
        w_row = [weights_ref[k : k + 1, :] for k in range(2)]
        f_row = forths_of(route)
        r_col, f_col = route_columns(r_row, f_row)
        slot_row = []
        for k in range(2):
            earlier = jnp.where((sub < lane) & ((r_col[0] == r_row[k]) | (r_col[1] == r_row[k])), 1.0, 0.0)
            slot_row.append(jnp.sum(earlier, axis=0, keepdims=True) + 1.0)
        info_col = [hops_of(r, f, z, x) for r, f in zip(r_col, f_col)]
        info_row = [hops_of(r, f, z, x) for r, f in zip(r_row, f_row)]
        kind = iota((8, TOK), 0)
        here = jnp.zeros((8, TOK), F32)
        for k in range(2):
            _, other, offset = info_row[k]
            value = jnp.where(kind < 2, slot_row[k], w_row[k])
            here = here + jnp.where((offset == 0) & (jnp.bitwise_and(kind, 1) == other) & (kind < 4), value, 0.0)
        meta_here[route] = here
        j = iota((16, TOK), 0)
        target = 2 * jnp.right_shift(j, 2) + jnp.bitwise_and(j, 1)
        is_slot = jnp.bitwise_and(j, 2) == 0
        orders = []
        for way in range(2):
            far_col = jnp.maximum(info_col[0][0][way], info_col[1][0][way])
            far_row = jnp.maximum(info_row[0][0][way], info_row[1][0][way])
            ahead_of_row = (far_col > far_row) | ((far_col == far_row) & (sub < lane))
            pos_row = jnp.sum(jnp.where(ahead_of_row, 1.0, 0.0), axis=0, keepdims=True)
            ahead_of_col = (far_row > far_col) | ((far_row == far_col) & (lane < sub))
            pos_col = jnp.sum(jnp.where(ahead_of_col, 1.0, 0.0), axis=1, keepdims=True)
            order = jnp.where(sub.astype(F32) == pos_row, 1.0, 0.0).astype(BF16)
            back[route, way] = jnp.where(lane.astype(F32) == pos_col, 1.0, 0.0).astype(BF16)
            meta = jnp.zeros((16, TOK), F32)
            for k in range(2):
                code = code_of(info_row[k][0][way], info_row[k][1])
                meta = meta + jnp.where(code == target, jnp.where(is_slot, slot_row[k], w_row[k]), 0.0)
            high = meta.astype(BF16)
            low = (meta - high.astype(F32)).astype(BF16)
            meta0[route, way] = dot_t(high, order) + dot_t(low, order)
            orders.append(order)
        return orders

    def scale_of(tokens):
        values = tokens[...].astype(F32)
        return lax.rsqrt(jnp.mean(values * values, axis=-1, keepdims=True) + EPS)

    def normalize(tokens, out):
        inv = scale_of(tokens)

        def body(cols):
            out[:, cols] = (tokens[:, cols].astype(F32) * inv * gain[:, cols]).astype(BF16)

        over_tiles(body)

    def pack(array, way, order, rows):
        def body(cols):
            packed[array, way, 0 : reach[0], cols] = dot(order[: reach[0]], rows[:, cols]).astype(BF16)

        over_tiles(body)

    def pick_here(array, route, rows):
        own, other = selector(meta_here.at[route], 0)
        both = jnp.concatenate([own, other], axis=0).astype(BF16)

        def body(cols):
            picked = dot(both, rows[:, cols]).astype(BF16)
            xin[array, 0:SLOTS, cols] = picked[:SLOTS]
            xsend[array, 0:SLOTS, cols] = picked[SLOTS:]

        over_tiles(body)
        cross(array, 0).start()

    def pick(array, route, ways, hop):
        block = block_of(ways[0], hop)
        rows = reach[hop - 1]
        at = pl.ds(block * SLOTS, SLOTS)
        matrices = []
        for way in ways:
            own, other = selector(metas[hop].at[route, way], 4 * (hop - 1))
            matrices.append(jnp.concatenate([own, other], axis=0)[:, :rows].astype(BF16))

        def body(cols):
            picked = sum(dot(m, landed(array, w, hop)[:, cols]) for m, w in zip(matrices, ways)).astype(BF16)
            xin[array, at, cols] = picked[:SLOTS]
            xsend[array, at, cols] = picked[SLOTS:]

        over_tiles(body)
        cross(array, block).start()

    def advance(array, hop, route=None):
        for way in range(2):
            if route is not None:
                meta_copy(route, way, hop).wait_recv()
                if hop < 4:
                    meta_copy(route, way, hop + 1).start()
            dispatch(array, way, hop).wait_recv()
            if hop < 4:
                dispatch(array, way, hop + 1).start()

    def pick_all(array, hop, route):
        if hop == 4:
            pick(array, route, (0, 1), 4)
        else:
            pick(array, route, (0,), hop)
            pick(array, route, (1,), hop)

    def spread(which, route, hop):
        rows = reach[hop - 1]
        further = reach[hop] if hop < 4 else 0
        blocks = [pl.ds(block_of(way, hop) * SLOTS, SLOTS) for way in range(2)]
        matrices = [spreader(metas[hop].at[route, way], 4 * (hop - 1))[:rows] for way in range(2)]
        for piece in range(PIECES):
            cols = piece_of(piece)
            for way, at, matrix in zip(range(2), blocks, matrices):
                own, other = outs[which][at, cols], outs_x[which][at, cols]
                total = dot(matrix, jnp.concatenate([own, other, own, other], axis=0))
                if further:
                    give_back(which, way, hop + 1, piece).wait_recv()
                    came = returned(which, way, hop + 1)[:, cols].astype(F32)
                    if further < rows:
                        came = jnp.concatenate([came, jnp.zeros((rows - further, width // PIECES), F32)], axis=0)
                    total = total + came
                landed(reused[which], way, hop)[:, cols] = total.astype(BF16)
                give_back(which, way, hop, piece).start()
        if which == 0:
            extra = pl.ds(width, TOK)
            for way, at in zip(range(2), blocks):
                own, other = selector(metas[hop].at[route, way], 4 * (hop - 1))
                scalars = scalar_rows(own, other, y_b[at, extra], yx_b[at, extra], hop)
                if hop < 4:
                    give_scalars(way, hop + 1).wait_recv()
                    scalars = scalars + ct_in[way, hop]
                ct_out[way, hop - 1] = scalars
                give_scalars(way, hop).start()

    def scalar_rows(own, other, mine, theirs, hop):
        row = iota((8, TOK), 0)
        first = jnp.sum(own * mine.astype(F32), axis=0, keepdims=True)
        second = jnp.sum(other * theirs.astype(F32), axis=0, keepdims=True)
        return jnp.where(row == 2 * (hop - 1), first, jnp.where(row == 2 * (hop - 1) + 1, second, 0.0))

    def gather_sums(which, route, use):
        matrix = spreader(meta_here.at[route], 0)
        orders = [back[route, way][:, : reach[0]] for way in range(2)]
        at = pl.ds(0, SLOTS)
        for piece in range(PIECES):
            cols = piece_of(piece)
            own, other = outs[which][at, cols], outs_x[which][at, cols]
            total = dot(matrix, jnp.concatenate([own, other, own, other], axis=0))
            for way in range(2):
                give_back(which, way, 1, piece).wait_recv()
                total = total + dot(orders[way], returned(which, way, 1)[:, cols])
            use(piece, cols, total)

    def backward_hidden(first, last):
        @pl.loop(first, last)
        def _(i):
            cols = pl.ds(pl.multiple_of(i * 256, 256), 256)
            gate = dot(xin[SAVED], w_gate[:, cols])
            up = dot(xin[SAVED], w_up[:, cols])
            back_in = dot_t(xin[GRAD], w_down[cols, :])
            sigmoid = jax.nn.sigmoid(gate)
            active = gate * sigmoid
            rounded = (active * up).astype(BF16).astype(F32)
            part = jnp.sum(rounded * back_in, axis=1, keepdims=True)
            hid_a[:, cols] = (back_in * up * sigmoid * (1.0 + gate * (1.0 - sigmoid))).astype(BF16)
            hid_b[:, cols] = (back_in * active).astype(BF16)
            res_part = jnp.broadcast_to(part, (part.shape[0], TOK))

            @pl.when(i == 0)
            def _():
                done_b[...] = res_part

            @pl.when(i > 0)
            def _():
                done_b[...] = done_b[...] + res_part

    def backward_rows():
        y_b[:, width : width + TOK] = done_b[...].astype(BF16)

        def body(cols):
            y_b[:, cols] = (dot_t(hid_a[...], w_gate[cols, :]) + dot_t(hid_b[...], w_up[cols, :])).astype(BF16)

        over_tiles(body)

    def forward_hidden():
        @pl.loop(0, hidden // 256)
        def _(i):
            cols = pl.ds(pl.multiple_of(i * 256, 256), 256)
            gate = dot(xin[FWD], w_gate[:, cols])
            up = dot(xin[FWD], w_up[:, cols])
            hid_a[:, cols] = (gate * jax.nn.sigmoid(gate) * up).astype(BF16)

    def forward_rows():
        def body(cols):
            y_f[:, cols] = dot(hid_a[...], w_down[:, cols]).astype(BF16)

        over_tiles(body)

    def start_cross_back(which, blocks):
        for block in blocks:
            cross_back(which, block).start()

    def wait_cross_back(which, blocks):
        for block in blocks:
            cross_back(which, block).wait_recv()

    orders_b = plan(BWD_ROUTE, routes_b, weights_b)
    loads[0].wait()
    for way in range(2):
        pack(GRAD, way, orders_b[way], grads)
    pl.semaphore_wait(barrier, 5)
    for way in range(2):
        dispatch(GRAD, way, 1).start()
    for way in range(2):
        meta_copy(BWD_ROUTE, way, 1).start()
    loads[1].wait()
    normalize(tokens_b, done_f)
    for way in range(2):
        pack(SAVED, way, orders_b[way], done_f)
        dispatch(SAVED, way, 1).start()
    pick_here(GRAD, BWD_ROUTE, grads)
    pick_here(SAVED, BWD_ROUTE, done_f)

    def prepare_forward():
        orders_f = plan(FWD_ROUTE, routes_f, weights_f)
        loads[2].wait()
        normalize(tokens_f, done_f)
        for way in range(2):
            meta_copy(FWD_ROUTE, way, 1).start()
            pack(FWD, way, orders_f[way], done_f)
        pick_here(FWD, FWD_ROUTE, done_f)

    for hop in range(1, 5):
        advance(GRAD, hop, BWD_ROUTE)
        pick_all(GRAD, hop, BWD_ROUTE)
        advance(SAVED, hop)
        if hop == 3:
            for way in range(2):
                dispatch(FWD, way, 1).start()
        pick_all(SAVED, hop, BWD_ROUTE)
        if hop == 1:
            prepare_forward()

    for load in loads[3:]:
        load.wait()
    for block in range(8):
        cross(SAVED, block).wait_recv()
        cross(GRAD, block).wait_recv()
    steps = hidden // 256
    backward_hidden(0, 1)
    advance(FWD, 1, FWD_ROUTE)
    pick_all(FWD, 1, FWD_ROUTE)
    backward_hidden(1, steps)
    backward_rows()
    start_cross_back(0, (LAST,))
    for hop in range(1, 5):
        for way in range(2):
            dispatch(SAVED, way, hop).wait_send()
    advance(FWD, 2, FWD_ROUTE)
    pick_all(FWD, 2, FWD_ROUTE)
    start_cross_back(0, (3, 6))
    wait_cross_back(0, (LAST,))
    spread(0, BWD_ROUTE, 4)
    advance(FWD, 3, FWD_ROUTE)
    pick_all(FWD, 3, FWD_ROUTE)
    wait_cross_back(0, (3, 6))
    spread(0, BWD_ROUTE, 3)
    advance(FWD, 4, FWD_ROUTE)
    pick_all(FWD, 4, FWD_ROUTE)
    start_cross_back(0, (2, 5))
    for block in range(8):
        cross(FWD, block).wait_recv()
    forward_hidden()
    wait_cross_back(0, (2, 5))
    spread(0, BWD_ROUTE, 2)
    forward_rows()
    start_cross_back(1, (LAST, 3, 6))
    start_cross_back(0, (1, 4, 0))
    start_cross_back(1, (2, 5, 1, 4, 0))
    for hop in range(1, 5):
        for way in range(2):
            dispatch(FWD, way, hop).wait_send()
    wait_cross_back(1, (LAST,))
    spread(1, FWD_ROUTE, 4)
    wait_cross_back(1, (3, 6))
    spread(1, FWD_ROUTE, 3)
    wait_cross_back(0, (1, 4, 0))
    spread(0, BWD_ROUTE, 1)
    wait_cross_back(1, (2, 5))
    spread(1, FWD_ROUTE, 2)

    def finish_backward():
        def keep(piece, cols, total):
            res[:, cols] = total

        gather_sums(0, BWD_ROUTE, keep)
        inv = scale_of(tokens_b)
        scaled = res[...] * gain[...]
        inner = jnp.mean(tokens_b[...].astype(F32) * scaled, axis=-1, keepdims=True)
        cubed = inv * inv * inv * inner

        def body(cols):
            values = tokens_b[:, cols].astype(F32)
            grad = grads[:, cols].astype(F32) + inv * (res[:, cols] * gain[:, cols]) - values * cubed
            packed[0, 0, :, cols] = grad.astype(BF16)

        for way in range(2):
            dispatch(GRAD, way, 1).wait_send()
        over_tiles(body)

    grad_out = remote(packed.at[0, 0], next_grad, s_send.at[0], s_recv.at[0], seg_prev)

    def input_out(piece):
        cols = piece_of(piece)
        at = 1 + piece
        return remote(packed.at[0, 1, :, cols], next_input.at[:, cols], s_send.at[at], s_recv.at[at], seg_next)

    finish_backward()
    grad_out.start()
    wait_cross_back(1, (1, 4, 0))
    spread(1, FWD_ROUTE, 1)

    own, other = selector(meta_here.at[BWD_ROUTE], 0)
    at = pl.ds(0, SLOTS)
    extra = pl.ds(width, TOK)
    local = scalar_rows(own, other, y_b[at, extra], yx_b[at, extra], 1)
    unit = jnp.where(lane == sub, 1.0, 0.0).astype(BF16)
    values = [dot_t(unit, local.astype(BF16))]
    for way in range(2):
        give_scalars(way, 1).wait_recv()
        values.append(dot_t(back[BWD_ROUTE, way], ct_in[way, 0].astype(BF16)))
    column = iota((TOK, 8), 1)
    picked = jnp.zeros((TOK, TOK), F32)
    columns = route_columns([routes_b[k : k + 1, :] for k in range(2)], forths_of(BWD_ROUTE))
    for k in range(2):
        hops, off_column, offset = hops_of(columns[0][k], columns[1][k], z, x)
        codes = [jnp.where(offset == 0, off_column, -1)] + [code_of(hop, off_column) for hop in hops]
        total = sum(jnp.where(code == column, value, 0.0) for code, value in zip(codes, values))
        picked = jnp.where(lane == k, jnp.sum(total, axis=1, keepdims=True), picked)
    combine[...] = jnp.transpose(picked)[:2, :].astype(BF16)

    def finish_forward(piece, cols, total):
        packed[0, 1, :, cols] = (tokens_f[:, cols].astype(F32) + total).astype(BF16)
        input_out(piece).start()

    gather_sums(1, FWD_ROUTE, finish_forward)

    for hop in range(1, 5):
        for way in range(2):
            if hop > 1:
                dispatch(GRAD, way, hop).wait_send()
            for route in range(2):
                meta_copy(route, way, hop).wait_send()
                for piece in range(PIECES):
                    give_back(route, way, hop, piece).wait_send()
            give_scalars(way, hop).wait_send()
    for block in range(8):
        for array in range(3):
            cross(array, block).wait_send()
        for which in range(2):
            cross_back(which, block).wait_send()
    for out in [grad_out] + [input_out(piece) for piece in range(PIECES)]:
        out.wait_send()
        out.wait_recv()


def hand_over(*refs):
    half = len(refs) // 2
    for source, target in zip(refs[:half], refs[half:]):
        target[...] = source[...]


def pass_through(number, rows, width, hidden):
    c1, c2, c3, c4 = TIERS[number]
    every = 16 * SLOTS
    vmem = pl.BlockSpec(memory_space=pltpu.VMEM)
    hbm = pl.BlockSpec(memory_space=pl.ANY)
    dma = pltpu.SemaphoreType.DMA
    meta = pltpu.VMEM((2, 2, 16, TOK), F32)
    return pl.pallas_call(
        functools.partial(kernel, TIERS[number], number == len(TIERS) - 1),
        out_shape=(
            jax.ShapeDtypeStruct((rows, width), BF16),
            jax.ShapeDtypeStruct((rows, width), BF16),
            jax.ShapeDtypeStruct((2, rows), BF16),
        ),
        in_specs=[vmem, hbm, vmem, vmem, hbm, vmem, vmem, hbm, vmem] + [hbm] * 3,
        out_specs=(vmem, vmem, vmem),
        scratch_shapes=[
            pltpu.VMEM((rows, width), BF16),
            pltpu.VMEM((rows, width), BF16),
            pltpu.VMEM((rows, width), BF16),
            pltpu.VMEM((3, 2, rows, width), BF16),
            pltpu.VMEM((3, 2, c1, width), BF16),
            pltpu.VMEM((3, 2, c2, width), BF16),
            pltpu.VMEM((3, 2, c3, width), BF16),
            pltpu.VMEM((3, 2 * c4, width), BF16),
            meta, meta, meta, meta, meta,
            pltpu.VMEM((2, 8, TOK), F32),
            pltpu.VMEM((2, 2, TOK, TOK), BF16),
            pltpu.VMEM((3, every // 2, width), BF16),
            pltpu.VMEM((3, every, width), BF16),
            pltpu.VMEM((width, hidden), BF16),
            pltpu.VMEM((width, hidden), BF16),
            pltpu.VMEM((hidden, width), BF16),
            pltpu.VMEM((every, hidden), BF16),
            pltpu.VMEM((every, hidden), BF16),
            pltpu.VMEM((every, width + TOK), BF16),
            pltpu.VMEM((every, width), BF16),
            pltpu.VMEM((every // 2, width + TOK), BF16),
            pltpu.VMEM((every // 2, width), BF16),
            pltpu.VMEM((2, 2, c1, width), BF16),
            pltpu.VMEM((2, 2, c2, width), BF16),
            pltpu.VMEM((2, 2, c3, width), BF16),
            pltpu.VMEM((2, 2 * c4, width), BF16),
            pltpu.VMEM((2, 4, 8, TOK), F32),
            pltpu.VMEM((2, 4, 8, TOK), F32),
            pltpu.VMEM((rows, width), F32),
            pltpu.VMEM((rows, width), BF16),
            pltpu.VMEM((every, TOK), F32),
            dma((3, 2, 4)), dma((3, 2, 4)),
            dma((2, 2, 4)), dma((2, 2, 4)),
            dma((3, 8)), dma((3, 8)),
            dma((2, 8)), dma((2, 8)),
            dma((2, 2, 4, PIECES)), dma((2, 2, 4, PIECES)),
            dma((2, 4)), dma((2, 4)),
            dma((1 + PIECES,)), dma((1 + PIECES,)),
            dma((6,)),
        ],
        compiler_params=pltpu.CompilerParams(
            collective_id=1 + number, has_side_effects=True, vmem_limit_bytes=60 * 1024 * 1024
        ),
        cost_estimate=pl.CostEstimate(
            flops=2 * every * width * hidden * 8, bytes_accessed=6 * width * hidden, transcendentals=2 * every * hidden
        ),
    )


def step(
    fwd_tokens, fwd_routes, fwd_weights, saved_tokens, bwd_routes, bwd_weights, incoming_grad, norm_gain,
    gate_proj, up_proj, down_proj,
):
    rows, width = fwd_tokens.shape[1:]
    hidden = gate_proj.shape[3]
    vmem = pl.BlockSpec(memory_space=pltpu.VMEM)
    dma = pltpu.SemaphoreType.DMA
    most = max(count for _, _, count in GROUPS)
    routes_f, routes_b = fwd_routes[0].T, bwd_routes[0].T
    table = jax.ShapeDtypeStruct((8, TOK), jnp.int32)
    plan, tier = pl.pallas_call(
        agree,
        out_shape=(table, table),
        in_specs=[vmem, vmem],
        out_specs=(vmem, vmem),
        scratch_shapes=[
            pltpu.VMEM((len(GROUPS), most, 8, TOK), F32),
            dma((len(GROUPS), most)), dma((len(GROUPS), most)),
        ],
        compiler_params=pltpu.CompilerParams(collective_id=0, has_side_effects=True),
    )(routes_b, routes_f)
    outs = lax.switch(
        tier[0, 0],
        [pass_through(number, rows, width, hidden) for number in range(len(TIERS))],
        plan, fwd_tokens[0], routes_f, fwd_weights[0].T, saved_tokens[0], routes_b, bwd_weights[0].T,
        incoming_grad[0], norm_gain, gate_proj[0, 0], up_proj[0, 0], down_proj[0, 0],
    )
    outs = pl.pallas_call(
        hand_over,
        out_shape=tuple(jax.ShapeDtypeStruct(out.shape, out.dtype) for out in outs),
        in_specs=[vmem] * 3,
        out_specs=(vmem,) * 3,
    )(*outs)
    return (outs[0][None], outs[1][None], outs[2].T[None])


def solution(mesh):
    rows = P("segment", "expert", None)
    return jax.shard_map(
        step,
        mesh=mesh,
        in_specs=(rows,) * 7 + (P("segment", None),) + (P("segment", "expert", None, None),) * 3,
        out_specs=(rows, rows, rows),
        check_vma=False,
    )
```

profile of v0, /device:TPU:1, one launch (start us, length us, event | category | flops | bytes accessed | tf_op | source)
XLA Modules:
  0.0 188.0 jit_solution(1229346120841103951)
XLA Ops:
  0.6 22.3 %shard_map.130 = (s32[8,128]{1,0:T(8,128)S(1)}, s32[8,128]{1,0:T(8,128)}) custom-call(s32[2,128]{1,0:T(2,128)} %bitcast.24, s32[2,128]{1,0:T(2,128)} %bitcast.27), custom_call_target="tpu_custom_call" | custom-call | tf_op jit(solution)/shard_map/pallas_call | solution.py:737
  22.9 1.2 slice.3
  24.8 162.2 %conditional.1 = ((bf16[128,2048]{1,0:T(8,128)(2,1)S(1)}, bf16[128,2048]{1,0:T(8,128)(2,1)S(1)}, bf16[2,128]{1,0:T(2,128)(2,1)S(1)})) conditional(s32[]{:T(128)} %bitcast.4, (s32[8,128]{1,0:T(8,128)S(1)}, bf16[128,2048]{1,0:T(8,128)(2,1)}, s32[2,128]{1,0:T(2,128)}, f32[2,128]{1,0:T(2,128)}, bf16[128,2048]{1,0:T(8,128)(2,1)}, ...), branch_computations={%region_0.0_spmd, %region_1.0_spmd} | conditional | flops 12884901888 | bytes 9437192 | solution.py:748
  24.8 162.0 %branch_0_fun.1 = (bf16[128,2048]{1,0:T(8,128)(2,1)S(1)}, bf16[128,2048]{1,0:T(8,128)(2,1)S(1)}, bf16[2,128]{1,0:T(2,128)(2,1)S(1)}) custom-call(s32[8,128]{1,0:T(8,128)S(1)} %get-tuple-element.48.plan_ref, bf16[128,2048]{1,0:T(8,128)(2,1)} %get-tuple-element.49.tokens_f_hbm, s32[2,128]{1,0:T(2,128)} %get-tuple-element.50.routes_f, ...), custom_call_target="tpu_custom_call" | custom-call | flops 12884901888 | bytes 9437184 | tf_op jit(solution)/shard_map/cond/branch_0_fun/pallas_call | solution.py:748
  187.0 1.0 shard_map.131
where the time goes:
time: 191 us; the launch traced here: 188 us
  Pallas kernels  185 us (97%)
    pallas_call x1, Pallas kernels, step(): lax.switch(tier[0, 0], [pass_through(number, rows, width, hidden) for num...  162 us
    pallas_call x1, Pallas kernels, step(): pl.pallas_call(agree, out_shape=(table, table), in_specs=[vmem, vmem], ou...  22.3 us

commit v1 on v0

--- a/solution.py
+++ b/solution.py
@@ -438,28 +438,32 @@
                 total = total + dot(orders[way], returned(which, way, 1)[:, cols])
             use(piece, cols, total)
 
-    def backward_hidden(first, last):
+    half_rows = 8 * SLOTS
+
+    def backward_hidden(half, first, last):
+        at = pl.ds(half * half_rows, half_rows)
+
         @pl.loop(first, last)
         def _(i):
             cols = pl.ds(pl.multiple_of(i * 256, 256), 256)
-            gate = dot(xin[SAVED], w_gate[:, cols])
-            up = dot(xin[SAVED], w_up[:, cols])
-            back_in = dot_t(xin[GRAD], w_down[cols, :])
+            gate = dot(xin[SAVED, at], w_gate[:, cols])
+            up = dot(xin[SAVED, at], w_up[:, cols])
+            back_in = dot_t(xin[GRAD, at], w_down[cols, :])
             sigmoid = jax.nn.sigmoid(gate)
             active = gate * sigmoid
             rounded = (active * up).astype(BF16).astype(F32)
             part = jnp.sum(rounded * back_in, axis=1, keepdims=True)
-            hid_a[:, cols] = (back_in * up * sigmoid * (1.0 + gate * (1.0 - sigmoid))).astype(BF16)
-            hid_b[:, cols] = (back_in * active).astype(BF16)
+            hid_a[at, cols] = (back_in * up * sigmoid * (1.0 + gate * (1.0 - sigmoid))).astype(BF16)
+            hid_b[at, cols] = (back_in * active).astype(BF16)
             res_part = jnp.broadcast_to(part, (part.shape[0], TOK))
 
             @pl.when(i == 0)
             def _():
-                done_b[...] = res_part
+                done_b[at, :] = res_part
 
             @pl.when(i > 0)
             def _():
-                done_b[...] = done_b[...] + res_part
+                done_b[at, :] = done_b[at, :] + res_part
 
     def backward_rows():
         y_b[:, width : width + TOK] = done_b[...].astype(BF16)
@@ -530,14 +534,14 @@
 
     for load in loads[3:]:
         load.wait()
+    steps = hidden // 256
+    backward_hidden(0, 0, steps)
     for block in range(8):
         cross(SAVED, block).wait_recv()
         cross(GRAD, block).wait_recv()
-    steps = hidden // 256
-    backward_hidden(0, 1)
     advance(FWD, 1, FWD_ROUTE)
     pick_all(FWD, 1, FWD_ROUTE)
-    backward_hidden(1, steps)
+    backward_hidden(1, 0, steps)
     backward_rows()
     start_cross_back(0, (LAST,))
     for hop in range(1, 5):

time: 191 us -> 189 us (0.990)
  no operation moved by 1% of the time
where the time goes in v1:
time: 189 us; the launch traced here: 187 us
  Pallas kernels  184 us (97%)
    pallas_call x1, Pallas kernels, step(): lax.switch(tier[0, 0], [pass_through(number, rows, width, hidden) for num...  161 us
    pallas_call x1, Pallas kernels, step(): pl.pallas_call(agree, out_shape=(table, table), in_specs=[vmem, vmem], ou...  22.3 us

profile of v1, /device:TPU:1, one launch (start us, length us, event | category | flops | bytes accessed | tf_op | source)
XLA Modules:
  0.0 187.0 jit_solution(11237410318010904414)
XLA Ops:
  0.6 22.3 %shard_map.130 = (s32[8,128]{1,0:T(8,128)S(1)}, s32[8,128]{1,0:T(8,128)}) custom-call(s32[2,128]{1,0:T(2,128)} %bitcast.24, s32[2,128]{1,0:T(2,128)} %bitcast.27), custom_call_target="tpu_custom_call" | custom-call | tf_op jit(solution)/shard_map/pallas_call | solution.py:741
  22.9 1.2 slice.3
  24.8 161.2 %conditional.1 = ((bf16[128,2048]{1,0:T(8,128)(2,1)S(1)}, bf16[128,2048]{1,0:T(8,128)(2,1)S(1)}, bf16[2,128]{1,0:T(2,128)(2,1)S(1)})) conditional(s32[]{:T(128)} %bitcast.4, (s32[8,128]{1,0:T(8,128)S(1)}, bf16[128,2048]{1,0:T(8,128)(2,1)}, s32[2,128]{1,0:T(2,128)}, f32[2,128]{1,0:T(2,128)}, bf16[128,2048]{1,0:T(8,128)(2,1)}, ...), branch_computations={%region_0.0_spmd, %region_1.0_spmd} | conditional | flops 12884901888 | bytes 9437192 | solution.py:752
  24.8 161.0 %branch_0_fun.1 = (bf16[128,2048]{1,0:T(8,128)(2,1)S(1)}, bf16[128,2048]{1,0:T(8,128)(2,1)S(1)}, bf16[2,128]{1,0:T(2,128)(2,1)S(1)}) custom-call(s32[8,128]{1,0:T(8,128)S(1)} %get-tuple-element.48.plan_ref, bf16[128,2048]{1,0:T(8,128)(2,1)} %get-tuple-element.49.tokens_f_hbm, s32[2,128]{1,0:T(2,128)} %get-tuple-element.50.routes_f, ...), custom_call_target="tpu_custom_call" | custom-call | flops 12884901888 | bytes 9437184 | tf_op jit(solution)/shard_map/cond/branch_0_fun/pallas_call | solution.py:752
  185.9 1.0 shard_map.131
